TPU v7x, 1024 devices: a whole 8x8x8 slice. The times are simulated.
1024 devices in a mesh: grp: 64 (over x_hi, z, core), exp: 16 (over y, x_lo).
Axes of the slice: x: 8 (x_hi: 4, x_lo: 2; x = x_hi * 2 + x_lo), y: 8, z: 8, core: 2. Of those that a mesh axis runs over, the one named last changes fastest.
Arguments:
- hidden: bfloat16 [64, 64, 7168], P('grp', 'exp'), may hold values from -6 to 6
- norm_gain: float32 [7168], replicated, may hold values from 0.1 to 1.9
- route: int32 [64, 64, 1], P('grp', 'exp'), may hold values from 0 to 1; in each aligned block of 4 rows (0 to 3, 4 to 7, ..., all dimensions but the last counted through in order) at most 3 rows name the same one
- route_weight: float32 [64, 64], P('grp', 'exp'), may hold values from 0.2 to 1
- resident: bfloat16 [2, 2048, 7168], P(None, 'exp'), may hold values from -0.0625 to 0.0625
- sectioned: bfloat16 [64, 512, 7168], P('grp', 'exp'), may hold values from -0.1875 to 0.1875
- owner: int32 [64], replicated, may hold values from 0 to 63, each once
Outputs:
- moe_out: bfloat16 [64, 64, 7168], P('grp', 'exp')
Inputs may be any that keep to these rules, and one draw needn't show every extreme that they name: `route`: each row names one of the 2 experts. Among the 4 rows of one device at most 3 name the same expert, and in every draw some device has exactly 3 rows naming one expert. Every group number appears exactly once, so the 4 buckets have distinct owner groups.
All inputs are finite; a program needn't handle non-finite values.
Results may differ from a plain program's by a relative error of at most 0.0071.
Values may be sent and summed in bfloat16 or wider, within the bound.
A program may use at most 32 MiB of HBM per device.

v0:
```python
import jax
import jax.numpy as jnp
from jax import lax
from jax.sharding import PartitionSpec as P

E_WIN = 2
BUCKETS = 4
CAP = 3


epsilon = 1e-06


def from_root(value, axis, source):
    kept = jnp.where(lax.axis_index(axis) == source, value, 0).astype(value.dtype)
    return lax.psum(kept, axis)


def activate(slot_rows, gate_up):
    gate_part = lax.dot_general(
        slot_rows, gate_up[0], (((1,), (1,)), ((), ())), preferred_element_type=jnp.float32
    )
    up_part = lax.dot_general(
        slot_rows, gate_up[1], (((1,), (1,)), ((), ())), preferred_element_type=jnp.float32
    )
    return (jax.nn.silu(gate_part) * up_part).astype(jnp.bfloat16)


def per_device(hidden, norm_gain, route, route_weight, resident, sectioned, owner):
    row_data = hidden[0].astype(jnp.float32)
    width = row_data.shape[1]
    row_count = row_data.shape[0]
    scale = lax.rsqrt(jnp.mean(row_data * row_data, axis=1, keepdims=True) + epsilon)
    normed = (row_data * scale * norm_gain[None, :]).astype(jnp.bfloat16)
    devices = lax.axis_size("exp")
    shards = devices // E_WIN
    expert_ids = route[0, :, 0]
    onehot = (expert_ids[:, None] == jnp.arange(E_WIN, dtype=jnp.int32)[None, :]).astype(jnp.int32)
    position = jnp.cumsum(onehot, axis=0) - onehot
    slot_index = jnp.sum(position * onehot, axis=1)
    placing = onehot[:, :, None] * (
        slot_index[:, None, None] == jnp.arange(CAP, dtype=jnp.int32)[None, None, :]
    ).astype(jnp.int32)
    placing = placing.reshape(row_count, E_WIN * CAP)
    packed = jnp.dot(
        placing.astype(jnp.bfloat16).T, normed, preferred_element_type=jnp.float32
    ).astype(jnp.bfloat16)
    packed = packed.reshape(E_WIN, 1, CAP, width)
    outgoing = jnp.broadcast_to(packed, (E_WIN, shards, CAP, width)).reshape(devices, CAP, width)
    fetched = []
    for bucket in range(BUCKETS):
        fetched.append(from_root(sectioned[0], "grp", owner[bucket]))
    down_rows = jnp.concatenate(fetched, axis=0)
    arrived = lax.all_to_all(outgoing, "exp", split_axis=0, concat_axis=0, tiled=True)
    flat_slots = arrived.reshape(-1, width)
    activation = activate(flat_slots, resident)
    partials = jnp.dot(activation, down_rows, preferred_element_type=jnp.float32)
    partials = partials.astype(jnp.bfloat16).reshape(arrived.shape)
    returned = lax.all_to_all(partials, "exp", split_axis=0, concat_axis=0, tiled=True)
    summed = jnp.sum(returned.astype(jnp.float32).reshape(E_WIN, shards, CAP, width), axis=1)
    summed = summed.reshape(E_WIN * CAP, width)
    combined = jnp.dot(placing.astype(jnp.float32), summed, precision=lax.Precision.HIGHEST)
    result = (combined * route_weight[0][:, None]).astype(jnp.bfloat16)
    return result.reshape(1, row_count, width)


def solution(mesh):
    in_specs = (
        P("grp", "exp", None),
        P(),
        P("grp", "exp", None),
        P("grp", "exp"),
        P(None, "exp", None),
        P("grp", "exp", None),
        P(),
    )
    out_specs = P("grp", "exp", None)
    return jax.shard_map(
        per_device, mesh=mesh, in_specs=in_specs, out_specs=out_specs, check_vma=False
    )
```

profile of v0, /device:TPU:10, one launch (start us, length us, event | category | flops | bytes accessed | tf_op | source)
XLA Modules:
  0.0 627.6 jit_solution(6790043437708524903)
XLA Ops:
  6.5 0.0 copy-start.1
  6.5 0.0 copy-start
  6.5 0.0 copy-start.3
  6.5 0.0 all-reduce.3.cloned.1.call-start
  6.5 1.5 fusion.42
  10.5 2.3 select_bitcast_fusion.3
  12.8 0.0 all-reduce.3.cloned.1.call-update
  12.9 0.0 copy-done.1
  12.9 0.1 fusion.38
  13.0 0.2 select_reduce_fusion
  13.2 0.1 fusion.39
  13.2 0.1 multiply_convert_fusion.1
  13.3 0.0 copy-done
  13.3 0.2 fusion.24
  13.5 0.1 convert_element_type.64
  13.6 0.0 copy-done.3
  13.6 0.2 convolution_convert_fusion.1
  13.9 0.1 broadcast_in_dim.20
  13.9 0.2 broadcast_in_dim.21
  14.2 33.9 %all_to_all.10 = bf16[16,3,7168]{2,1,0:T(4,128)(2,1)S(1)} all-to-all(bf16[16,3,7168]{2,1,0:T(4,128)(2,1)S(1)} %bitcast.47), channel_id=1, replica_groups=mesh['grp'=64,'exp'=16] {'exp'}, dimensions={0} | all-to-all | bytes 1376256 | tf_op jit(solution)/shard_map/all_to_all | solution.py:54
  48.0 0.6 reshape.122
  48.6 2.2 fusion.12
  50.9 532.3 %all-reduce.3.cloned.1.call-done = (bf16[32,7168]{1,0:T(8,128)(2,1)}, bf16[32,7168]{1,0:T(8,128)(2,1)}, bf16[32,7168]{1,0:T(8,128)(2,1)}, bf16[32,7168]{1,0:T(8,128)(2,1)}) async-done(((bf16[32,7168]{1,0:T(8,128)(2,1)}, bf16[32,7168]{1,0:T(8,128)(2,1)}, bf16[32,7168]{1,0:T(8,128)(2,1)}, bf16[32,7168]{1,0:T(8,128)(2,1)}), (bf16[32,7168]{1,0:T(8,128)(2,1)}, bf16[32,7168]{1,0:T(8,128)(2,1)}, ...) | async-done | bytes 1835024 | tf_op jit(solution)/shard_map/psum | solution.py:16
  583.2 3.4 convolution_convert_fusion
  586.6 0.0 copy-start.2
  586.6 0.4 reshape.123
  587.1 32.2 %all_to_all.11 = bf16[16,3,7168]{2,1,0:T(4,128)(2,1)S(1)} all-to-all(bf16[16,3,7168]{2,1,0:T(4,128)(2,1)S(1)} %reshape.123), channel_id=1, replica_groups=mesh['grp'=64,'exp'=16] {'exp'}, dimensions={0} | all-to-all | bytes 1376256 | tf_op jit(solution)/shard_map/all_to_all | solution.py:59
  619.3 0.4 convert_reduce_fusion
  619.7 0.0 copy-done.2
  619.7 1.1 fusion.2
  (2 shorter events, 0.0 us)
Async XLA Ops:
  6.5 6.3 %copy-start.1 = (s32[1,4,1]{1,2,0:T(1,128)S(1)}, s32[1,4,1]{1,2,0:T(1,128)}, u32[]{:S(2)}) copy-start(s32[1,4,1]{1,2,0:T(1,128)} %param.9) | copy-start | bytes 52
  6.5 6.8 %copy-start = (bf16[1,4,7168]{2,1,0:T(4,128)(2,1)S(1)}, bf16[1,4,7168]{2,1,0:T(4,128)(2,1)}, u32[]{:S(2)}) copy-start(bf16[1,4,7168]{2,1,0:T(4,128)(2,1)} %param.7) | copy-start | bytes 172036
  6.5 7.1 %copy-start.3 = (f32[7168]{0:T(1024)S(1)}, f32[7168]{0:T(1024)}, u32[]{:S(2)}) copy-start(f32[7168]{0:T(1024)} %param.8) | copy-start | bytes 86020
  6.5 576.6 %all-reduce.3.cloned.1.call-start = ((), (), s32[]{:S(2)}) async-start(), calls=%async_computation.2 | async-start | bytes 3670016 | tf_op jit(solution)/shard_map/psum | solution.py:16
  586.6 33.1 %copy-start.2 = (f32[1,4]{1,0:T(1,128)S(1)}, f32[1,4]{1,0:T(1,128)}, u32[]{:S(2)}) copy-start(f32[1,4]{1,0:T(1,128)} %param.10) | copy-start | bytes 52
Sparse Core Ops, SparseCore 0:
  13.0 570.1 all-reduce.2
where the time goes:
time: 628 us
  waiting for transfers between devices  532 us (85%)
  blocking collectives  66.1 us (11%)
  between operations  16 us (3%)
  matrix products  7 us (1%)
    psum x1, waiting for transfers between devices, from_root(): return lax.psum(kept, axis)  532 us
    all_to_all x1, blocking collectives, per_device(): lax.all_to_all(outgoing, 'exp', split_axis=0, concat_axis=0, tiled=True)  33.9 us
    all_to_all x1, blocking collectives, per_device(): lax.all_to_all(partials, 'exp', split_axis=0, concat_axis=0, tiled=True)  32.2 us
  transfers between devices with their start and end apart: 1, of which 1 were waited for; matrix products, arithmetic and copies ran while one was open for 1% of the time, Pallas kernels for 0%

commit v1 on v0

v1 whole, which is shorter than its diff:
```python
import jax
import jax.numpy as jnp
from jax import lax
from jax.experimental import pallas as pl
from jax.experimental.pallas import tpu as pltpu
from jax.sharding import PartitionSpec as P

MESH = pl.DeviceIdType.MESH
BUCKETS = 4
EPSILON = 1e-06
XH, Z, Y = 4, 8, 8
HALF = 4
ZW = 7
SUB = 16
COLS = 256
QUARTER = ZW * COLS
FLAG = 128


def kernel(
    owner, hidden, gain, route, weight, resident, sectioned,
    out,
    gate_up, staged, rows, perm, chunks, chosen, down, act, acts, product, sends, partials, sums, finals, gathered,
    local_sem, row_send, row_recv, a_send, a_recv, a_local, w_send, w_recv, w_local, act_send, act_recv, act_local,
    y_send, y_recv, y_local, z_send, z_recv, z_local,
):
    g, e = lax.axis_index("grp"), lax.axis_index("exp")
    xh, z, c = g // 16, (g // 2) % 8, g % 2
    y, xl = e // 2, e % 2
    half, quarter = y // HALF, y % HALF

    def wait_for(blocks, sem):
        pltpu.make_async_copy(chunks.at[pl.ds(0, blocks)], chunks.at[pl.ds(0, blocks)], sem).wait()

    def grp(a, b, d):
        return (a * Z + b) * 2 + d

    load = pltpu.make_async_copy(resident, gate_up, local_sem)
    load.start()

    barrier = pltpu.get_barrier_semaphore()

    def greet(gg, ee):
        pl.semaphore_signal(barrier, inc=1, device_id=(gg, ee), device_id_type=MESH)

    def greet_plane(i, carry):
        greet((g + i) % 64, e)
        return carry

    def greet_exp(i, carry):
        greet(g, (e + i) % 16)
        return carry

    def greet_acts(i, carry):
        greet(grp(xh, (z + 1 + i % 7) % Z, c), (half * HALF + (quarter + 1 + i // 7) % HALF) * 2 + xl)
        return carry

    def greet_down(i, carry):
        k = (xh * 2 + c + 1 + i % 7) % 8
        greet(grp(k // 2, z, k % 2), (half * HALF + (quarter + 1 + i // 7) % HALF) * 2 + xl)
        return carry

    lax.fori_loop(1, 64, greet_plane, 0)
    lax.fori_loop(1, 16, greet_exp, 0)
    lax.fori_loop(0, 21, greet_acts, 0)
    lax.fori_loop(0, 21, greet_down, 0)

    data = hidden[...].astype(jnp.float32)
    scale = lax.rsqrt(jnp.mean(data * data, axis=1, keepdims=True) + EPSILON)
    normed = data * scale * gain[...]
    flags = jnp.broadcast_to(route[...].astype(jnp.float32), (4, FLAG))
    for j in range(4):
        staged[4 * j : 4 * j + 4, 0:QUARTER] = normed[:, j * QUARTER : (j + 1) * QUARTER]
        staged[4 * j : 4 * j + 4, QUARTER:] = flags
    rows[e] = staged[...].astype(jnp.bfloat16)

    to = lax.broadcasted_iota(jnp.int32, (256, 256), 0)
    source = lax.broadcasted_iota(jnp.int32, (256, 256), 1)
    wanted = ((to % 64) // 4) * 16 + (to // 64) * 4 + to % 4
    perm[...] = jnp.where(wanted == source, 1.0, 0.0).astype(jnp.bfloat16)

    pl.semaphore_wait(barrier, 63 + 15 + 21 + 21)

    def slot(dy, other):
        return ((y + dy + 8) % 8) * 2 + (1 - xl if other else xl)

    def pass_on(s, ee):
        pltpu.make_async_remote_copy(
            src_ref=rows.at[s], dst_ref=rows.at[s], send_sem=row_send, recv_sem=row_recv.at[s],
            device_id=(g, ee), device_id_type=MESH,
        ).start()

    def row_wait(s):
        pltpu.make_async_copy(rows.at[s], rows.at[s], row_recv.at[s]).wait()

    right, left, across = slot(1, False), slot(-1, False), slot(0, True)
    pass_on(e, across)
    pass_on(e, right)
    pass_on(e, left)

    def a_dest(i):
        k = (xh * 2 + c + i // 8) % 8
        zz = (z + i % 8) % 8
        return k // 2, zz, k % 2

    def a_source(aa, zz, cc):
        column = pl.multiple_of(aa * QUARTER + zz * COLS, 128)
        return sectioned.at[pl.ds(pl.multiple_of(cc * SUB, SUB), SUB), pl.ds(column, COLS)]

    def a_start(i, carry):
        aa, zz, cc = a_dest(i)

        @pl.when(zz < ZW)
        def _():
            pltpu.make_async_remote_copy(
                src_ref=a_source(aa, zz, cc), dst_ref=chunks.at[g], send_sem=a_send, recv_sem=a_recv,
                device_id=(grp(aa, zz, cc), e), device_id_type=MESH,
            ).start()

        return carry

    @pl.when(z < ZW)
    def _():
        pltpu.make_async_copy(a_source(xh, z, c), chunks.at[g], a_local).start()

    lax.fori_loop(1, 64, a_start, 0)

    row_wait(across)
    pass_on(across, right)
    pass_on(across, left)
    for d in (1, 2, 3):
        for other in (False, True):
            s = slot(-d, other)
            row_wait(s)
            if d < 3 or not other:
                pass_on(s, right)
            s = slot(d, other)
            row_wait(s)
            if d < 3 or other:
                pass_on(s, left)
    row_wait(slot(4, False))
    row_wait(slot(4, True))

    load.wait()
    flat = rows[...].reshape(256, QUARTER + FLAG)
    ordered = jnp.dot(perm[...], flat, preferred_element_type=jnp.float32).astype(jnp.bfloat16)
    gates = jnp.zeros((64, 128), jnp.float32)
    ups = jnp.zeros((64, 128), jnp.float32)
    for j in range(4):
        part = ordered[j * 64 : (j + 1) * 64, 0:QUARTER]
        lanes = slice(j * QUARTER, (j + 1) * QUARTER)
        gates += lax.dot_general(
            part, gate_up[0, :, lanes], (((1,), (1,)), ((), ())), preferred_element_type=jnp.float32
        )
        ups += lax.dot_general(
            part, gate_up[1, :, lanes], (((1,), (1,)), ((), ())), preferred_element_type=jnp.float32
        )
    expert = ordered[0:64, QUARTER:].astype(jnp.float32)
    mine = jnp.abs(expert - half.astype(jnp.float32)) < 0.5
    act[...] = jnp.where(mine, jax.nn.silu(gates) * ups, 0.0).astype(jnp.bfloat16)

    def act_place():
        return acts.at[z, :, pl.ds(pl.multiple_of(quarter * 128, 128), 128)]

    def act_start(i, carry):
        zz = (z + i % 8) % 8
        ee = (half * HALF + (quarter + i // 8) % HALF) * 2 + xl

        @pl.when(zz < ZW)
        def _():
            pltpu.make_async_remote_copy(
                src_ref=act, dst_ref=act_place(), send_sem=act_send, recv_sem=act_recv,
                device_id=(grp(xh, zz, c), ee), device_id_type=MESH,
            ).start()

        return carry

    @pl.when(z < ZW)
    def _():
        pltpu.make_async_copy(act, act_place(), act_local).start()

    lax.fori_loop(1, 32, act_start, 0)

    @pl.when(z < ZW)
    def _():
        pltpu.make_async_copy(a_source(xh, z, c), chunks.at[g], a_local).wait()
        wait_for(63, a_recv)
        for b in range(BUCKETS):
            chosen[b] = chunks[owner[b]]

        yy = half * HALF + xh
        place = down.at[quarter, :, c]

        @pl.when(xh == quarter)
        def _():
            pltpu.make_async_copy(chosen, place, w_local).start()

        for i in range(8):
            k = (xh * 2 + c + i) % 8

            def w_start():
                pltpu.make_async_remote_copy(
                    src_ref=chosen, dst_ref=place, send_sem=w_send, recv_sem=w_recv,
                    device_id=(grp(k // 2, z, k % 2), yy * 2 + xl), device_id_type=MESH,
                ).start()

            if i == 0:
                pl.when(xh != quarter)(w_start)
            else:
                w_start()

        pltpu.make_async_copy(act, act_place(), act_local).wait()
        wait_for(62, act_recv)

        @pl.when(xh == quarter)
        def _():
            wait_for(28, w_recv)
            pltpu.make_async_copy(chosen, place, w_local).wait()

        @pl.when(xh != quarter)
        def _():
            wait_for(32, w_recv)

        product[...] = jnp.dot(
            acts[...].reshape(512, 512), down[...].reshape(512, COLS), preferred_element_type=jnp.float32
        )
        for ee in range(16):
            for zz in range(8):
                sends[ee * 32 + zz * 4 : ee * 32 + zz * 4 + 4, :] = product[zz * 64 + ee * 4 : zz * 64 + ee * 4 + 4, :]
        gathered[...] = sends[...].astype(jnp.bfloat16).reshape(16, 32, COLS)

        def y_start(i, carry):
            ee = (e + i) % 16
            pltpu.make_async_remote_copy(
                src_ref=gathered.at[ee], dst_ref=partials.at[e], send_sem=y_send, recv_sem=y_recv,
                device_id=(g, ee), device_id_type=MESH,
            ).start()
            return carry

        lax.fori_loop(1, 16, y_start, 0)
        own = pltpu.make_async_copy(gathered.at[e], partials.at[e], y_local)
        own.start()
        own.wait()
        wait_for(30, y_recv)
        for q in range(4):
            total = jnp.zeros((32, COLS), jnp.float32)
            for hh in range(2):
                for ll in range(2):
                    total += partials[(hh * HALF + q) * 2 + ll].astype(jnp.float32)
            product[q * 32 : q * 32 + 32, :] = total
        for q in range(4):
            for zz in range(8):
                sends[zz * 16 + q * 4 : zz * 16 + q * 4 + 4, :] = product[q * 32 + zz * 4 : q * 32 + zz * 4 + 4, :]
        sums[...] = sends[0:128, :].astype(jnp.bfloat16).reshape(8, 16, COLS)

        for i in range(1, 8):
            zz = (z + i) % 8
            pltpu.make_async_remote_copy(
                src_ref=sums.at[zz], dst_ref=finals.at[z], send_sem=z_send, recv_sem=z_recv,
                device_id=(grp(xh, zz, c), e), device_id_type=MESH,
            ).start()
        own_z = pltpu.make_async_copy(sums.at[z], finals.at[z], z_local)
        own_z.start()
        own_z.wait()

    @pl.when(z < ZW)
    def _():
        wait_for(6, z_recv)

    @pl.when(z == ZW)
    def _():
        wait_for(7, z_recv)

    scaled = weight[...]
    sends[0 : ZW * SUB, :] = finals[0:ZW].astype(jnp.float32).reshape(ZW * SUB, COLS)
    for zz in range(ZW):
        for q in range(4):
            lanes = slice(q * QUARTER + zz * COLS, q * QUARTER + (zz + 1) * COLS)
            out[:, lanes] = (sends[zz * 16 + q * 4 : zz * 16 + q * 4 + 4, :] * scaled).astype(jnp.bfloat16)

    pltpu.make_async_copy(rows.at[pl.ds(0, 15)], rows.at[pl.ds(0, 15)], row_send).wait()

    @pl.when(z == ZW)
    def _():
        wait_for(56, a_send)
        wait_for(56, act_send)

    @pl.when(z < ZW)
    def _():
        wait_for(55, a_send)
        wait_for(54, act_send)
        wait_for(30, y_send)
        wait_for(7, z_send)

        @pl.when(xh == quarter)
        def _():
            wait_for(28, w_send)

        @pl.when(xh != quarter)
        def _():
            wait_for(32, w_send)


def per_device(hidden, norm_gain, route, route_weight, resident, sectioned, owner):
    width = hidden.shape[-1]
    vmem, anywhere = pl.BlockSpec(memory_space=pltpu.VMEM), pl.BlockSpec(memory_space=pl.ANY)
    half = lambda *shape: pltpu.VMEM(shape, jnp.bfloat16)
    single = lambda *shape: pltpu.VMEM(shape, jnp.float32)
    dma = pltpu.SemaphoreType.DMA
    result = pl.pallas_call(
        kernel,
        out_shape=jax.ShapeDtypeStruct((4, width), jnp.bfloat16),
        in_specs=[pl.BlockSpec(memory_space=pltpu.SMEM), vmem, vmem, vmem, vmem, anywhere, anywhere],
        out_specs=vmem,
        scratch_shapes=[
            half(2, 128, width),
            single(SUB, QUARTER + FLAG),
            half(16, SUB, QUARTER + FLAG),
            half(256, 256),
            half(64, SUB, COLS),
            half(BUCKETS, SUB, COLS),
            half(4, BUCKETS, 2, SUB, COLS),
            half(64, 128),
            half(8, 64, 512),
            single(512, COLS),
            single(512, COLS),
            half(16, 32, COLS),
            half(8, SUB, COLS),
            half(8, SUB, COLS),
            half(16, 32, COLS),
            dma, dma, dma((16,)), dma, dma, dma, dma, dma, dma, dma, dma, dma, dma, dma, dma, dma, dma, dma,
        ],
        compiler_params=pltpu.CompilerParams(
            collective_id=0, has_side_effects=True, vmem_limit_bytes=40 * 2**20
        ),
    )(
        owner,
        hidden[0],
        norm_gain[None, :],
        route[0],
        route_weight.reshape(4, 1),
        resident,
        sectioned[0],
    )
    return result[None]


def solution(mesh):
    in_specs = (
        P("grp", "exp", None),
        P(),
        P("grp", "exp", None),
        P("grp", "exp"),
        P(None, "exp", None),
        P("grp", "exp", None),
        P(),
    )
    return jax.shard_map(
        per_device, mesh=mesh, in_specs=in_specs, out_specs=P("grp", "exp", None), check_vma=False
    )
```

time: 628 us -> 84.7 us (0.13)
  the two profiles are of different devices: /device:TPU:10 before, /device:TPU:2 now
where the time goes in v1:
time: 84.7 us; the launch traced here: 84.4 us
  Pallas kernels  77 us (91%)
  local copies, waits for them, and re-layouts  7.38 us (9%)
    pallas_call x1, Pallas kernels, per_device(): pl.pallas_call(kernel, out_shape=jax.ShapeDtypeStruct((4, width), jnp.bfl...  77 us
    unnamed x11, local copies, waits for them, and re-layouts  5.9 us

profile of v1, /device:TPU:2, one launch (start us, length us, event | category | flops | bytes accessed | tf_op | source)
XLA Modules:
  0.0 84.4 jit_solution(5916455758532382627)
XLA Ops:
  0.0 0.7 copy.8.route
  0.7 0.7 copy.9.weight
  1.5 0.0 copy-start
  1.5 2.0 %copy-done = bf16[2,128,7168]{2,1,0:T(8,128)(2,1)S(1)} copy-done((bf16[2,128,7168]{2,1,0:T(8,128)(2,1)S(1)}, bf16[2,128,7168]{2,1,0:T(8,128)(2,1)}, u32[]{:S(2)}) %copy-start) | copy-done | bytes 3670040
  3.5 0.0 copy-start.1
  3.5 1.0 %copy-done.1 = bf16[1,32,7168]{2,1,0:T(8,128)(2,1)S(1)} copy-done((bf16[1,32,7168]{2,1,0:T(8,128)(2,1)S(1)}, bf16[1,32,7168]{2,1,0:T(8,128)(2,1)}, u32[]{:S(2)}) %copy-start.1) | copy-done | bytes 458776
  4.5 0.0 copy-start.2
  4.5 0.8 copy-done.2
  5.4 0.0 copy-start.3
  5.4 0.7 copy-done.3
  6.1 0.0 copy-start.4
  6.1 0.7 copy-done.4
  6.8 77.0 %shard_map.73 = bf16[4,7168]{1,0:T(4,128)(2,1)S(1)} custom-call(s32[64]{0:T(128)S(1)} %copy-done.4, bf16[4,7168]{1,0:T(4,128)(2,1)S(1)} %bitcast.8, f32[1,7168]{1,0:T(1,128)S(1)} %bitcast.9, s32[4,1]{1,0:T(4,128)S(1)} %copy.8.route, f32[4,1]{1,0:T(4,128)S(1)} %copy.9.weight, bf16[2,128,7168]{2,1,0:T(8,128)(2,1)S(1)} %copy-done, bf16[32,7168]{1,0:T(8,128)(2,1)S(1)} %bitcast.6), custom_call_target="tpu_custom_call" | custom-call | tf_op jit(solution)/shard_map/pallas_call | solution.py:310
  83.8 0.6 copy.11
Async XLA Ops:
  1.5 2.0 %copy-start = (bf16[2,128,7168]{2,1,0:T(8,128)(2,1)S(1)}, bf16[2,128,7168]{2,1,0:T(8,128)(2,1)}, u32[]{:S(2)}) copy-start(bf16[2,128,7168]{2,1,0:T(8,128)(2,1)} %resident.1) | copy-start | bytes 11010052
  3.5 1.0 %copy-start.1 = (bf16[1,32,7168]{2,1,0:T(8,128)(2,1)S(1)}, bf16[1,32,7168]{2,1,0:T(8,128)(2,1)}, u32[]{:S(2)}) copy-start(bf16[1,32,7168]{2,1,0:T(8,128)(2,1)} %param.12) | copy-start | bytes 1376260
  4.5 0.8 copy-start.2
  5.4 0.7 copy-start.3
  6.1 0.7 copy-start.4

commit v2 on v1

--- a/solution.py
+++ b/solution.py
@@ -68,7 +68,11 @@
     data = hidden[...].astype(jnp.float32)
     scale = lax.rsqrt(jnp.mean(data * data, axis=1, keepdims=True) + EPSILON)
     normed = data * scale * gain[...]
-    flags = jnp.broadcast_to(route[...].astype(jnp.float32), (4, FLAG))
+    line = lax.broadcasted_iota(jnp.int32, (4, FLAG), 0)
+    flags = jnp.zeros((4, FLAG), jnp.int32)
+    for r in range(4):
+        flags = jnp.where(line == r, route[r], flags)
+    flags = flags.astype(jnp.float32)
     for j in range(4):
         staged[4 * j : 4 * j + 4, 0:QUARTER] = normed[:, j * QUARTER : (j + 1) * QUARTER]
         staged[4 * j : 4 * j + 4, QUARTER:] = flags
@@ -271,7 +275,10 @@
     def _():
         wait_for(7, z_recv)
 
-    scaled = weight[...]
+    line = lax.broadcasted_iota(jnp.int32, (4, COLS), 0)
+    scaled = jnp.zeros((4, COLS), jnp.float32)
+    for r in range(4):
+        scaled = jnp.where(line == r, weight[r], scaled)
     sends[0 : ZW * SUB, :] = finals[0:ZW].astype(jnp.float32).reshape(ZW * SUB, COLS)
     for zz in range(ZW):
         for q in range(4):
@@ -304,13 +311,14 @@
 def per_device(hidden, norm_gain, route, route_weight, resident, sectioned, owner):
     width = hidden.shape[-1]
     vmem, anywhere = pl.BlockSpec(memory_space=pltpu.VMEM), pl.BlockSpec(memory_space=pl.ANY)
+    smem = pl.BlockSpec(memory_space=pltpu.SMEM)
     half = lambda *shape: pltpu.VMEM(shape, jnp.bfloat16)
     single = lambda *shape: pltpu.VMEM(shape, jnp.float32)
     dma = pltpu.SemaphoreType.DMA
     result = pl.pallas_call(
         kernel,
         out_shape=jax.ShapeDtypeStruct((4, width), jnp.bfloat16),
-        in_specs=[pl.BlockSpec(memory_space=pltpu.SMEM), vmem, vmem, vmem, vmem, anywhere, anywhere],
+        in_specs=[smem, vmem, vmem, smem, smem, anywhere, anywhere],
         out_specs=vmem,
         scratch_shapes=[
             half(2, 128, width),
@@ -331,14 +339,14 @@
             dma, dma, dma((16,)), dma, dma, dma, dma, dma, dma, dma, dma, dma, dma, dma, dma, dma, dma, dma,
         ],
         compiler_params=pltpu.CompilerParams(
-            collective_id=0, has_side_effects=True, vmem_limit_bytes=40 * 2**20
+            collective_id=0, has_side_effects=True, vmem_limit_bytes=60 * 2**20
         ),
     )(
         owner,
         hidden[0],
         norm_gain[None, :],
-        route[0],
-        route_weight.reshape(4, 1),
+        route.reshape(4),
+        route_weight.reshape(4),
         resident,
         sectioned[0],
     )

time: 84.7 us -> 79.1 us (0.934)
  the two profiles are of different devices: /device:TPU:2 before, /device:TPU:10 now
where the time goes in v2:
time: 79.1 us; the launch traced here: 78.9 us
  Pallas kernels  77.4 us (98%)
  local copies, waits for them, and re-layouts  1.46 us (2%)
    pallas_call x1, Pallas kernels, per_device(): pl.pallas_call(kernel, out_shape=jax.ShapeDtypeStruct((4, width), jnp.bfl...  77.4 us

profile of v2, /device:TPU:10, one launch (start us, length us, event | category | flops | bytes accessed | tf_op | source)
XLA Modules:
  0.0 78.9 jit_solution(5334027089510074189)
XLA Ops:
  0.0 77.4 %shard_map.73 = bf16[4,7168]{1,0:T(4,128)(2,1)} custom-call(s32[64]{0:T(128)} %owner.1, bf16[4,7168]{1,0:T(4,128)(2,1)} %bitcast.8, f32[1,7168]{1,0:T(1,128)} %bitcast.9, s32[4]{0:T(128)} %bitcast.10, f32[4]{0:T(128)} %bitcast.11, bf16[2,128,7168]{2,1,0:T(8,128)(2,1)} %resident.1, bf16[32,7168]{1,0:T(8,128)(2,1)} %bitcast.6), custom_call_target="tpu_custom_call" | custom-call | tf_op jit(solution)/shard_map/pallas_call | solution.py:318
  77.4 1.5 %copy.9 = bf16[1,4,7168]{2,1,0:T(4,128)(2,1)} copy(bf16[1,4,7168]{2,1,0:T(4,128)(2,1)} %bitcast.7) | data formatting | bytes 114688

commit v3 on v2

--- a/solution.py
+++ b/solution.py
@@ -15,12 +15,14 @@
 COLS = 256
 QUARTER = ZW * COLS
 FLAG = 128
+SLOTS = 48
 
 
 def kernel(
     owner, hidden, gain, route, weight, resident, sectioned,
     out,
-    gate_up, staged, rows, perm, chunks, chosen, down, act, acts, product, sends, partials, sums, finals, gathered,
+    gate_up, staged, rows, perm, spread, merge, chunks, chosen, down, act, acts, packed, parts, full,
+    partials, sums, finals, gathered,
     local_sem, row_send, row_recv, a_send, a_recv, a_local, w_send, w_recv, w_local, act_send, act_recv, act_local,
     y_send, y_recv, y_local, z_send, z_recv, z_local,
 ):
@@ -32,6 +34,10 @@
     def wait_for(blocks, sem):
         pltpu.make_async_copy(chunks.at[pl.ds(0, blocks)], chunks.at[pl.ds(0, blocks)], sem).wait()
 
+    def wait_slots(blocks, sem):
+        ref = gate_up.at[0, pl.ds(0, SLOTS), pl.ds(0, blocks * 128)]
+        pltpu.make_async_copy(ref, ref, sem).wait()
+
     def grp(a, b, d):
         return (a * Z + b) * 2 + d
 
@@ -68,20 +74,42 @@
     data = hidden[...].astype(jnp.float32)
     scale = lax.rsqrt(jnp.mean(data * data, axis=1, keepdims=True) + EPSILON)
     normed = data * scale * gain[...]
-    line = lax.broadcasted_iota(jnp.int32, (4, FLAG), 0)
-    flags = jnp.zeros((4, FLAG), jnp.int32)
+    zeros = 4 - (route[0] + route[1] + route[2] + route[3])
+    place_of, seen0, seen1 = [], 0, zeros
     for r in range(4):
-        flags = jnp.where(line == r, route[r], flags)
-    flags = flags.astype(jnp.float32)
+        place_of.append(jnp.where(route[r] == 0, seen0, seen1))
+        seen0, seen1 = seen0 + 1 - route[r], seen1 + route[r]
+    line = lax.broadcasted_iota(jnp.int32, normed.shape, 0)
+    ranked = jnp.zeros_like(normed)
+    for r in range(4):
+        ranked = jnp.where(line == place_of[r], jnp.broadcast_to(normed[r : r + 1], normed.shape), ranked)
+    normed = ranked
+    flags = jnp.where(lax.broadcasted_iota(jnp.int32, (4, FLAG), 0) >= zeros, 1.0, 0.0)
     for j in range(4):
         staged[4 * j : 4 * j + 4, 0:QUARTER] = normed[:, j * QUARTER : (j + 1) * QUARTER]
         staged[4 * j : 4 * j + 4, QUARTER:] = flags
     rows[e] = staged[...].astype(jnp.bfloat16)
 
-    to = lax.broadcasted_iota(jnp.int32, (256, 256), 0)
-    source = lax.broadcasted_iota(jnp.int32, (256, 256), 1)
-    wanted = ((to % 64) // 4) * 16 + (to // 64) * 4 + to % 4
-    perm[...] = jnp.where(wanted == source, 1.0, 0.0).astype(jnp.bfloat16)
+    def ones(shape, wanted):
+        source = lax.broadcasted_iota(jnp.int32, shape, 1)
+        return jnp.where(wanted == source, 1.0, 0.0)
+
+    t = lax.broadcasted_iota(jnp.int32, (4 * SLOTS, 256), 0)
+    j4 = jnp.where(t >= SLOTS, 1, 0) + jnp.where(t >= 2 * SLOTS, 1, 0) + jnp.where(t >= 3 * SLOTS, 1, 0)
+    u = t - SLOTS * j4
+    dev = (u * 43) >> 7
+    perm[...] = ones((4 * SLOTS, 256), dev * 16 + j4 * 4 + (u - 3 * dev) + half).astype(jnp.bfloat16)
+    t = lax.broadcasted_iota(jnp.int32, (8 * SLOTS, 8 * SLOTS), 0)
+    dev = (t * 2731) >> 16
+    u = t - 24 * dev
+    zz = (u * 43) >> 7
+    spread[...] = ones((8 * SLOTS, 8 * SLOTS), zz * SLOTS + dev * 3 + (u - 3 * zz)).astype(jnp.bfloat16)
+    t = lax.broadcasted_iota(jnp.int32, (128, 4 * SLOTS), 0)
+    k = t % 4
+    base = ((t // 4) % 4) * SLOTS + (t // 16) * 3 + k
+    first = ones((128, 4 * SLOTS), jnp.where(k < 3, base, -1))
+    second = ones((128, 4 * SLOTS), jnp.where(k > 0, base + 23, -1))
+    merge[...] = (first + second).astype(jnp.bfloat16)
 
     pl.semaphore_wait(barrier, 63 + 15 + 21 + 21)
 
@@ -148,10 +176,10 @@
     load.wait()
     flat = rows[...].reshape(256, QUARTER + FLAG)
     ordered = jnp.dot(perm[...], flat, preferred_element_type=jnp.float32).astype(jnp.bfloat16)
-    gates = jnp.zeros((64, 128), jnp.float32)
-    ups = jnp.zeros((64, 128), jnp.float32)
+    gates = jnp.zeros((SLOTS, 128), jnp.float32)
+    ups = jnp.zeros((SLOTS, 128), jnp.float32)
     for j in range(4):
-        part = ordered[j * 64 : (j + 1) * 64, 0:QUARTER]
+        part = ordered[j * SLOTS : (j + 1) * SLOTS, 0:QUARTER]
         lanes = slice(j * QUARTER, (j + 1) * QUARTER)
         gates += lax.dot_general(
             part, gate_up[0, :, lanes], (((1,), (1,)), ((), ())), preferred_element_type=jnp.float32
@@ -159,7 +187,7 @@
         ups += lax.dot_general(
             part, gate_up[1, :, lanes], (((1,), (1,)), ((), ())), preferred_element_type=jnp.float32
         )
-    expert = ordered[0:64, QUARTER:].astype(jnp.float32)
+    expert = ordered[0:SLOTS, QUARTER:].astype(jnp.float32)
     mine = jnp.abs(expert - half.astype(jnp.float32)) < 0.5
     act[...] = jnp.where(mine, jax.nn.silu(gates) * ups, 0.0).astype(jnp.bfloat16)
 
@@ -214,7 +242,7 @@
                 w_start()
 
         pltpu.make_async_copy(act, act_place(), act_local).wait()
-        wait_for(62, act_recv)
+        wait_slots(31, act_recv)
 
         @pl.when(xh == quarter)
         def _():
@@ -225,13 +253,16 @@
         def _():
             wait_for(32, w_recv)
 
-        product[...] = jnp.dot(
-            acts[...].reshape(512, 512), down[...].reshape(512, COLS), preferred_element_type=jnp.float32
-        )
+        product = jnp.dot(
+            acts[...].reshape(8 * SLOTS, 512), down[...].reshape(512, COLS), preferred_element_type=jnp.float32
+        ).astype(jnp.bfloat16)
+        by_dev = jnp.dot(spread[...], product, preferred_element_type=jnp.float32)
         for ee in range(16):
-            for zz in range(8):
-                sends[ee * 32 + zz * 4 : ee * 32 + zz * 4 + 4, :] = product[zz * 64 + ee * 4 : zz * 64 + ee * 4 + 4, :]
-        gathered[...] = sends[...].astype(jnp.bfloat16).reshape(16, 32, COLS)
+            for k in range(2):
+                packed[ee * SLOTS + k * 24 : ee * SLOTS + k * 24 + 24, :] = by_dev[
+                    ee * 24 : ee * 24 + 24, k * 128 : (k + 1) * 128
+                ]
+        gathered[...] = packed[...].astype(jnp.bfloat16).reshape(16, SLOTS, 128)
 
         def y_start(i, carry):
             ee = (e + i) % 16
@@ -245,17 +276,17 @@
         own = pltpu.make_async_copy(gathered.at[e], partials.at[e], y_local)
         own.start()
         own.wait()
-        wait_for(30, y_recv)
+        wait_slots(15, y_recv)
         for q in range(4):
-            total = jnp.zeros((32, COLS), jnp.float32)
             for hh in range(2):
-                for ll in range(2):
-                    total += partials[(hh * HALF + q) * 2 + ll].astype(jnp.float32)
-            product[q * 32 : q * 32 + 32, :] = total
-        for q in range(4):
-            for zz in range(8):
-                sends[zz * 16 + q * 4 : zz * 16 + q * 4 + 4, :] = product[q * 32 + zz * 4 : q * 32 + zz * 4 + 4, :]
-        sums[...] = sends[0:128, :].astype(jnp.bfloat16).reshape(8, 16, COLS)
+                source = (hh * HALF + q) * 2
+                total = partials[source].astype(jnp.float32) + partials[source + 1].astype(jnp.float32)
+                for k in range(2):
+                    parts[q * SLOTS + hh * 24 : q * SLOTS + hh * 24 + 24, k * 128 : (k + 1) * 128] = total[
+                        k * 24 : k * 24 + 24
+                    ]
+        merged = jnp.dot(merge[...], parts[...].astype(jnp.bfloat16), preferred_element_type=jnp.float32)
+        sums[...] = merged.astype(jnp.bfloat16).reshape(8, 16, COLS)
 
         for i in range(1, 8):
             zz = (z + i) % 8
@@ -275,28 +306,32 @@
     def _():
         wait_for(7, z_recv)
 
-    line = lax.broadcasted_iota(jnp.int32, (4, COLS), 0)
-    scaled = jnp.zeros((4, COLS), jnp.float32)
-    for r in range(4):
-        scaled = jnp.where(line == r, weight[r], scaled)
-    sends[0 : ZW * SUB, :] = finals[0:ZW].astype(jnp.float32).reshape(ZW * SUB, COLS)
+    parts[0 : ZW * SUB, :] = finals[0:ZW].astype(jnp.float32).reshape(ZW * SUB, COLS)
     for zz in range(ZW):
         for q in range(4):
             lanes = slice(q * QUARTER + zz * COLS, q * QUARTER + (zz + 1) * COLS)
-            out[:, lanes] = (sends[zz * 16 + q * 4 : zz * 16 + q * 4 + 4, :] * scaled).astype(jnp.bfloat16)
+            full[:, lanes] = parts[zz * 16 + q * 4 : zz * 16 + q * 4 + 4, :]
+    line = lax.broadcasted_iota(jnp.int32, full.shape, 0)
+    result = jnp.zeros(full.shape, jnp.float32)
+    for k in range(4):
+        share = jnp.zeros(full.shape, jnp.float32)
+        for r in range(4):
+            share = jnp.where(line == r, jnp.where(place_of[r] == k, weight[r], 0.0), share)
+        result += share * full[k : k + 1, :]
+    out[...] = result.astype(jnp.bfloat16)
 
     pltpu.make_async_copy(rows.at[pl.ds(0, 15)], rows.at[pl.ds(0, 15)], row_send).wait()
 
     @pl.when(z == ZW)
     def _():
         wait_for(56, a_send)
-        wait_for(56, act_send)
+        wait_slots(28, act_send)
 
     @pl.when(z < ZW)
     def _():
         wait_for(55, a_send)
-        wait_for(54, act_send)
-        wait_for(30, y_send)
+        wait_slots(27, act_send)
+        wait_slots(15, y_send)
         wait_for(7, z_send)
 
         @pl.when(xh == quarter)
@@ -324,18 +359,21 @@
             half(2, 128, width),
             single(SUB, QUARTER + FLAG),
             half(16, SUB, QUARTER + FLAG),
-            half(256, 256),
+            half(4 * SLOTS, 256),
+            half(8 * SLOTS, 8 * SLOTS),
+            half(128, 4 * SLOTS),
             half(64, SUB, COLS),
             half(BUCKETS, SUB, COLS),
             half(4, BUCKETS, 2, SUB, COLS),
-            half(64, 128),
-            half(8, 64, 512),
-            single(512, COLS),
-            single(512, COLS),
-            half(16, 32, COLS),
+            half(SLOTS, 128),
+            half(8, SLOTS, 512),
+            single(16 * SLOTS, 128),
+            single(4 * SLOTS, COLS),
+            single(4, width),
+            half(16, SLOTS, 128),
             half(8, SUB, COLS),
             half(8, SUB, COLS),
-            half(16, 32, COLS),
+            half(16, SLOTS, 128),
             dma, dma, dma((16,)), dma, dma, dma, dma, dma, dma, dma, dma, dma, dma, dma, dma, dma, dma, dma,
         ],
         compiler_params=pltpu.CompilerParams(

time: 79.1 us -> 75.1 us (0.949)
  the two profiles are of different devices: /device:TPU:10 before, /device:TPU:1 now
where the time goes in v3:
time: 75.1 us; the launch traced here: 74.8 us
  Pallas kernels  73.3 us (98%)
  local copies, waits for them, and re-layouts  1.46 us (2%)
    pallas_call x1, Pallas kernels, per_device(): pl.pallas_call(kernel, out_shape=jax.ShapeDtypeStruct((4, width), jnp.bfl...  73.3 us

profile of v3, /device:TPU:1, one launch (start us, length us, event | category | flops | bytes accessed | tf_op | source)
XLA Modules:
  0.0 74.8 jit_solution(4920609310976441980)
XLA Ops:
  0.0 73.3 %shard_map.73 = bf16[4,7168]{1,0:T(4,128)(2,1)} custom-call(s32[64]{0:T(128)} %owner.1, bf16[4,7168]{1,0:T(4,128)(2,1)} %bitcast.8, f32[1,7168]{1,0:T(1,128)} %bitcast.9, s32[4]{0:T(128)} %bitcast.10, f32[4]{0:T(128)} %bitcast.11, bf16[2,128,7168]{2,1,0:T(8,128)(2,1)} %resident.1, bf16[32,7168]{1,0:T(8,128)(2,1)} %bitcast.6), custom_call_target="tpu_custom_call" | custom-call | tf_op jit(solution)/shard_map/pallas_call | solution.py:353
  73.4 1.5 %copy.9 = bf16[1,4,7168]{2,1,0:T(4,128)(2,1)} copy(bf16[1,4,7168]{2,1,0:T(4,128)(2,1)} %bitcast.7) | data formatting | bytes 114688

commit v4 on v3

--- a/solution.py
+++ b/solution.py
@@ -21,7 +21,7 @@
 def kernel(
     owner, hidden, gain, route, weight, resident, sectioned,
     out,
-    gate_up, staged, rows, perm, spread, merge, chunks, chosen, down, act, acts, packed, parts, full,
+    gate_up, staged, rows, perm, spread, merge, chunks, chosen, down, act, acts, packed, parts,
     partials, sums, finals, gathered,
     local_sem, row_send, row_recv, a_send, a_recv, a_local, w_send, w_recv, w_local, act_send, act_recv, act_local,
     y_send, y_recv, y_local, z_send, z_recv, z_local,
@@ -90,6 +90,52 @@
         staged[4 * j : 4 * j + 4, QUARTER:] = flags
     rows[e] = staged[...].astype(jnp.bfloat16)
 
+    pl.semaphore_wait(barrier, 63 + 15 + 21 + 21)
+
+    def slot(dy, other):
+        return ((y + dy + 8) % 8) * 2 + (1 - xl if other else xl)
+
+    def pass_on(s, ee):
+        pltpu.make_async_remote_copy(
+            src_ref=rows.at[s], dst_ref=rows.at[s], send_sem=row_send, recv_sem=row_recv.at[s],
+            device_id=(g, ee), device_id_type=MESH,
+        ).start()
+
+    def row_wait(s):
+        pltpu.make_async_copy(rows.at[s], rows.at[s], row_recv.at[s]).wait()
+
+    right, left, across = slot(1, False), slot(-1, False), slot(0, True)
+    pass_on(e, across)
+    pass_on(e, right)
+    pass_on(e, left)
+
+    def a_dest(i):
+        k = (xh * 2 + c + i // 8) % 8
+        zz = (z + i % 8) % 8
+        return k // 2, zz, k % 2
+
+    def a_source(aa, zz, cc):
+        column = pl.multiple_of(aa * QUARTER + zz * COLS, 128)
+        return sectioned.at[pl.ds(pl.multiple_of(cc * SUB, SUB), SUB), pl.ds(column, COLS)]
+
+    def a_start(i, carry):
+        aa, zz, cc = a_dest(i)
+
+        @pl.when(zz < ZW)
+        def _():
+            pltpu.make_async_remote_copy(
+                src_ref=a_source(aa, zz, cc), dst_ref=chunks.at[g], send_sem=a_send, recv_sem=a_recv,
+                device_id=(grp(aa, zz, cc), e), device_id_type=MESH,
+            ).start()
+
+        return carry
+
+    @pl.when(z < ZW)
+    def _():
+        pltpu.make_async_copy(a_source(xh, z, c), chunks.at[g], a_local).start()
+
+    lax.fori_loop(1, 64, a_start, 0)
+
     def ones(shape, wanted):
         source = lax.broadcasted_iota(jnp.int32, shape, 1)
         return jnp.where(wanted == source, 1.0, 0.0)
@@ -99,63 +145,6 @@
     u = t - SLOTS * j4
     dev = (u * 43) >> 7
     perm[...] = ones((4 * SLOTS, 256), dev * 16 + j4 * 4 + (u - 3 * dev) + half).astype(jnp.bfloat16)
-    t = lax.broadcasted_iota(jnp.int32, (8 * SLOTS, 8 * SLOTS), 0)
-    dev = (t * 2731) >> 16
-    u = t - 24 * dev
-    zz = (u * 43) >> 7
-    spread[...] = ones((8 * SLOTS, 8 * SLOTS), zz * SLOTS + dev * 3 + (u - 3 * zz)).astype(jnp.bfloat16)
-    t = lax.broadcasted_iota(jnp.int32, (128, 4 * SLOTS), 0)
-    k = t % 4
-    base = ((t // 4) % 4) * SLOTS + (t // 16) * 3 + k
-    first = ones((128, 4 * SLOTS), jnp.where(k < 3, base, -1))
-    second = ones((128, 4 * SLOTS), jnp.where(k > 0, base + 23, -1))
-    merge[...] = (first + second).astype(jnp.bfloat16)
-
-    pl.semaphore_wait(barrier, 63 + 15 + 21 + 21)
-
-    def slot(dy, other):
-        return ((y + dy + 8) % 8) * 2 + (1 - xl if other else xl)
-
-    def pass_on(s, ee):
-        pltpu.make_async_remote_copy(
-            src_ref=rows.at[s], dst_ref=rows.at[s], send_sem=row_send, recv_sem=row_recv.at[s],
-            device_id=(g, ee), device_id_type=MESH,
-        ).start()
-
-    def row_wait(s):
-        pltpu.make_async_copy(rows.at[s], rows.at[s], row_recv.at[s]).wait()
-
-    right, left, across = slot(1, False), slot(-1, False), slot(0, True)
-    pass_on(e, across)
-    pass_on(e, right)
-    pass_on(e, left)
-
-    def a_dest(i):
-        k = (xh * 2 + c + i // 8) % 8
-        zz = (z + i % 8) % 8
-        return k // 2, zz, k % 2
-
-    def a_source(aa, zz, cc):
-        column = pl.multiple_of(aa * QUARTER + zz * COLS, 128)
-        return sectioned.at[pl.ds(pl.multiple_of(cc * SUB, SUB), SUB), pl.ds(column, COLS)]
-
-    def a_start(i, carry):
-        aa, zz, cc = a_dest(i)
-
-        @pl.when(zz < ZW)
-        def _():
-            pltpu.make_async_remote_copy(
-                src_ref=a_source(aa, zz, cc), dst_ref=chunks.at[g], send_sem=a_send, recv_sem=a_recv,
-                device_id=(grp(aa, zz, cc), e), device_id_type=MESH,
-            ).start()
-
-        return carry
-
-    @pl.when(z < ZW)
-    def _():
-        pltpu.make_async_copy(a_source(xh, z, c), chunks.at[g], a_local).start()
-
-    lax.fori_loop(1, 64, a_start, 0)
 
     row_wait(across)
     pass_on(across, right)
@@ -213,6 +202,26 @@
 
     lax.fori_loop(1, 32, act_start, 0)
 
+    t = lax.broadcasted_iota(jnp.int32, (8 * SLOTS, 8 * SLOTS), 0)
+    dev = (t * 2731) >> 16
+    u = t - 24 * dev
+    zz = (u * 43) >> 7
+    spread[...] = ones((8 * SLOTS, 8 * SLOTS), zz * SLOTS + dev * 3 + (u - 3 * zz)).astype(jnp.bfloat16)
+    t = lax.broadcasted_iota(jnp.int32, (128, 4 * SLOTS), 0)
+    k = t % 4
+    base = ((t // 4) % 4) * SLOTS + (t // 16) * 3 + k
+    first = ones((128, 4 * SLOTS), jnp.where(k < 3, base, -1))
+    second = ones((128, 4 * SLOTS), jnp.where(k > 0, base + 23, -1))
+    merge[...] = (first + second).astype(jnp.bfloat16)
+
+    line = lax.broadcasted_iota(jnp.int32, (4, COLS), 0)
+    shares = []
+    for k in range(4):
+        share = jnp.zeros((4, COLS), jnp.float32)
+        for r in range(4):
+            share = jnp.where(line == r, jnp.where(place_of[r] == k, weight[r], 0.0), share)
+        shares.append(share)
+
     @pl.when(z < ZW)
     def _():
         pltpu.make_async_copy(a_source(xh, z, c), chunks.at[g], a_local).wait()
@@ -310,15 +319,11 @@
     for zz in range(ZW):
         for q in range(4):
             lanes = slice(q * QUARTER + zz * COLS, q * QUARTER + (zz + 1) * COLS)
-            full[:, lanes] = parts[zz * 16 + q * 4 : zz * 16 + q * 4 + 4, :]
-    line = lax.broadcasted_iota(jnp.int32, full.shape, 0)
-    result = jnp.zeros(full.shape, jnp.float32)
-    for k in range(4):
-        share = jnp.zeros(full.shape, jnp.float32)
-        for r in range(4):
-            share = jnp.where(line == r, jnp.where(place_of[r] == k, weight[r], 0.0), share)
-        result += share * full[k : k + 1, :]
-    out[...] = result.astype(jnp.bfloat16)
+            block = parts[zz * 16 + q * 4 : zz * 16 + q * 4 + 4, :]
+            total = shares[0] * block[0:1]
+            for k in range(1, 4):
+                total += shares[k] * block[k : k + 1]
+            out[:, lanes] = total.astype(jnp.bfloat16)
 
     pltpu.make_async_copy(rows.at[pl.ds(0, 15)], rows.at[pl.ds(0, 15)], row_send).wait()
 
@@ -369,7 +374,6 @@
             half(8, SLOTS, 512),
             single(16 * SLOTS, 128),
             single(4 * SLOTS, COLS),
-            single(4, width),
             half(16, SLOTS, 128),
             half(8, SUB, COLS),
             half(8, SUB, COLS),

time: 75.1 us -> 75.2 us (level)
  the two profiles are of different devices: /device:TPU:1 before, /device:TPU:10 now
where the time goes in v4:
time: 75.2 us; the launch traced here: 75 us
  Pallas kernels  73.5 us (98%)
  local copies, waits for them, and re-layouts  1.46 us (2%)
    pallas_call x1, Pallas kernels, per_device(): pl.pallas_call(kernel, out_shape=jax.ShapeDtypeStruct((4, width), jnp.bfl...  73.5 us

profile of v4, /device:TPU:10, one launch (start us, length us, event | category | flops | bytes accessed | tf_op | source)
XLA Modules:
  0.0 75.0 jit_solution(16470925990564901045)
XLA Ops:
  0.0 73.5 %shard_map.73 = bf16[4,7168]{1,0:T(4,128)(2,1)} custom-call(s32[64]{0:T(128)} %owner.1, bf16[4,7168]{1,0:T(4,128)(2,1)} %bitcast.8, f32[1,7168]{1,0:T(1,128)} %bitcast.9, s32[4]{0:T(128)} %bitcast.10, f32[4]{0:T(128)} %bitcast.11, bf16[2,128,7168]{2,1,0:T(8,128)(2,1)} %resident.1, bf16[32,7168]{1,0:T(8,128)(2,1)} %bitcast.6), custom_call_target="tpu_custom_call" | custom-call | tf_op jit(solution)/shard_map/pallas_call | solution.py:358
  73.5 1.5 %copy.9 = bf16[1,4,7168]{2,1,0:T(4,128)(2,1)} copy(bf16[1,4,7168]{2,1,0:T(4,128)(2,1)} %bitcast.7) | data formatting | bytes 114688
